TPU v7x, 32 devices: a whole 2x2x4 slice. The times are simulated.
32 devices in a mesh: group: 2 (over y), dp: 4 (over z), tensor: 4 (over x, core).
Axes of the slice: x: 2, y: 2, z: 4, core: 2. Of those that a mesh axis runs over, the one named last changes fastest.
Arguments:
- hidden: bfloat16 [4096, 4096], P(('group', 'dp')), parts along dimension 0, may hold values from -400 to 400
- lengths: int32 [64], P(('group', 'dp')), parts along dimension 0, may hold values from 1 to 255, as said below
- assignment: int32 [64], P(('group', 'dp')), parts along dimension 0, may hold values from 0 to 3, as said below
- norm_gain: bfloat16 [4096], replicated, may hold values from 0.5 to 1.5
- q_weight: bfloat16 [4096, 2048], P(None, 'tensor'), may hold values from -0.09375 to 0.09375
- q_bias: bfloat16 [2048], P('tensor'), may hold values from -3 to 3
- k_weight: bfloat16 [4096, 512], P(None, 'tensor'), may hold values from -0.09375 to 0.09375
- k_bias: bfloat16 [512], P('tensor'), may hold values from -4 to 4
- v_weight: bfloat16 [4096, 512], P(None, 'tensor'), may hold values from -0.09375 to 0.09375
- v_bias: bfloat16 [512], P('tensor'), may hold values from -4 to 4
- prompt_keys: bfloat16 [16384, 512], P(('group', 'dp'), 'tensor'), parts along dimension 0, may hold values from -310 to 310
- prompt_values: bfloat16 [16384, 512], P(('group', 'dp'), 'tensor'), parts along dimension 0, may hold values from -6 to 6
Outputs:
- attention: bfloat16 [4096, 2048], P(('group', 'dp'), 'tensor'), parts along dimension 0
There are 2 independent parts, one for each index of `group`. A program takes and returns all parts, laid end to end along the dimension named above; an argument that names none is the same for every part. Nothing has to cross between parts.
Inputs may be any that keep to these rules, and one draw needn't show every extreme that they name: The 8 lengths of one index of dp sum to exactly 512. `assignment`: each index of dp assigns exactly two of its responses to every index of dp, itself included, and the two have at most 256 rows together; in every draw one index of dp receives exactly 256 rows from every index of dp.
All inputs are finite; a program needn't handle non-finite values.
Results may differ from a plain program's by a relative error of at most 0.0055.
The roundings to bfloat16 on the way count: a program that leaves them out, or rounds other values in their place, can miss the bound.
Values may be sent and summed in bfloat16 or wider, within the bound.
A program may use at most 128 MiB of HBM per device.

v0:
```python
import jax
import jax.numpy as jnp
from jax import lax
from jax.sharding import PartitionSpec as P

PLEN = 2048


rope_base = 1000000.0
norm_eps = 1e-06


def rotate(lin_values, position, head_size):
    half_size = head_size // 2
    freqs = rope_base ** (-(jnp.arange(half_size, dtype=jnp.float32) * 2.0) / head_size)
    angles = position.astype(jnp.float32)[:, None] * freqs[None, :]
    cosine = jnp.cos(angles)[:, None, :]
    sine = jnp.sin(angles)[:, None, :]
    first_half = lin_values[..., :half_size]
    second_half = lin_values[..., half_size:]
    return jnp.concatenate(
        [first_half * cosine - second_half * sine, second_half * cosine + first_half * sine],
        axis=-1,
    )


def response_tables(resp_lengths, resp_dest):
    ordinal = jnp.arange(resp_lengths.shape[0], dtype=jnp.int32)
    starts = jnp.cumsum(resp_lengths) - resp_lengths
    same_dest = resp_dest[:, None] == resp_dest[None, :]
    earlier = ordinal[None, :] < ordinal[:, None]
    offsets = jnp.sum(jnp.where(same_dest & earlier, resp_lengths[None, :], 0), axis=1)
    return (starts, offsets)


def slot_owner(resp_lengths, resp_dest, slot_dest, within):
    starts, offsets = response_tables(resp_lengths, resp_dest)
    ordinal = jnp.arange(resp_lengths.shape[0], dtype=jnp.int32)
    matches = (
        (resp_dest[None, :] == slot_dest[:, None])
        & (offsets[None, :] <= within[:, None])
        & (within[:, None] < (offsets + resp_lengths)[None, :])
    )
    occupied = jnp.any(matches, axis=1)
    owner_id = jnp.where(occupied, jnp.sum(jnp.where(matches, ordinal[None, :], 0), axis=1), -1)
    place_in = within - jnp.sum(jnp.where(matches, offsets[None, :], 0), axis=1)
    home_row = jnp.sum(jnp.where(matches, starts[None, :], 0), axis=1) + place_in
    return (owner_id, place_in, home_row, occupied)


def home_slots(resp_lengths, resp_dest, slot_size, total_rows):
    starts, offsets = response_tables(resp_lengths, resp_dest)
    row_ids = jnp.arange(total_rows, dtype=jnp.int32)
    member = (row_ids[:, None] >= starts[None, :]) & (
        row_ids[:, None] < (starts + resp_lengths)[None, :]
    )
    place_in = row_ids - jnp.sum(jnp.where(member, starts[None, :], 0), axis=1)
    target = (
        jnp.sum(jnp.where(member, (resp_dest * slot_size + offsets)[None, :], 0), axis=1) + place_in
    )
    return (place_in, target)


def project(row_block, params):
    norm_gain, q_weight, q_bias, k_weight, k_bias, v_weight, v_bias = params
    widened = row_block.astype(jnp.float32)
    scale_row = lax.rsqrt(jnp.mean(widened * widened, axis=1, keepdims=True) + norm_eps)
    normed = (widened * scale_row * norm_gain.astype(jnp.float32)).astype(jnp.bfloat16)
    q_lin = jnp.dot(normed, q_weight, preferred_element_type=jnp.float32) + q_bias.astype(
        jnp.float32
    )
    k_lin = jnp.dot(normed, k_weight, preferred_element_type=jnp.float32) + k_bias.astype(
        jnp.float32
    )
    v_lin = jnp.dot(normed, v_weight, preferred_element_type=jnp.float32) + v_bias.astype(
        jnp.float32
    )
    return (q_lin, k_lin, v_lin)


def finish(joined, position, head_cols, head_size):
    row_count = joined.shape[0]
    q_lin = joined[:, :head_cols].reshape(row_count, head_cols // head_size, head_size)
    k_lin = joined[:, head_cols : head_cols + head_size].reshape(row_count, 1, head_size)
    queries = rotate(q_lin, position, head_size).astype(jnp.bfloat16)
    keys_rot = rotate(k_lin, position, head_size).astype(jnp.bfloat16).reshape(row_count, head_size)
    values_out = joined[:, head_cols + head_size :].astype(jnp.bfloat16)
    return (queries, keys_rot, values_out)


def local(
    hidden,
    lengths,
    assignment,
    norm_gain,
    q_weight,
    q_bias,
    k_weight,
    k_bias,
    v_weight,
    v_bias,
    prompt_keys,
    prompt_values,
):
    rank_count = lax.axis_size("dp")
    rank_here = lax.axis_index("dp")
    home_rows = hidden.shape[0]
    slot_size = 2 * home_rows // rank_count
    buffer_rows = rank_count * slot_size
    head_size = k_weight.shape[1]
    head_cols = q_weight.shape[1]
    heads_here = head_cols // head_size
    per_rank = lengths.shape[0]
    params = (norm_gain, q_weight, q_bias, k_weight, k_bias, v_weight, v_bias)
    ledger_lengths, ledger_dest = (
        lax.all_gather(lengths, "dp", axis=0, tiled=True),
        lax.all_gather(assignment, "dp", axis=0, tiled=True),
    )
    within = jnp.arange(slot_size, dtype=jnp.int32)
    to_here = jnp.zeros((slot_size,), jnp.int32) + rank_here

    def incoming_slots(source_lengths, source_dest):
        return slot_owner(source_lengths, source_dest, to_here, within)

    owner_ids, in_place, unused_rows, unused_found = jax.vmap(incoming_slots)(
        ledger_lengths.reshape(rank_count, per_rank), ledger_dest.reshape(rank_count, per_rank)
    )
    source_ids = jnp.arange(rank_count, dtype=jnp.int32)[:, None]
    slot_tags = jnp.where(owner_ids >= 0, source_ids * per_rank + owner_ids, -1).reshape(
        buffer_rows
    )
    slot_pos = (PLEN + in_place).reshape(buffer_rows)
    slot_ids = jnp.arange(buffer_rows, dtype=jnp.int32)
    unused_owner, unused_place, send_rows, send_found = slot_owner(
        lengths, assignment, slot_ids // slot_size, slot_ids % slot_size
    )
    home_place, home_target = home_slots(lengths, assignment, slot_size, home_rows)
    home_q, home_k, home_v = finish(
        jnp.concatenate(project(hidden, params), axis=1), PLEN + home_place, head_cols, head_size
    )
    joined = jnp.concatenate([home_q.reshape(home_rows, head_cols), home_k, home_v], axis=1)
    picked = jnp.take(joined, send_rows, axis=0)
    filled = jnp.where(send_found[:, None], picked, jnp.zeros((), joined.dtype))
    arrived = lax.all_to_all(
        filled.reshape(rank_count, slot_size, joined.shape[1]),
        "dp",
        split_axis=0,
        concat_axis=0,
        tiled=True,
    ).reshape(buffer_rows, -1)
    queries = arrived[:, :head_cols].reshape(buffer_rows, heads_here, head_size)
    keys_rot = arrived[:, head_cols : head_cols + head_size]
    values_out = arrived[:, head_cols + head_size :]
    block_rows = min(512, buffer_rows)
    block_count = buffer_rows // block_rows
    score_scale = head_size ** (-0.5)

    def attend(block_data):
        q_blk, k_blk, v_blk, tag_blk, pos_blk = block_data
        cached_scores = (
            jnp.einsum("qhd,kd->hqk", q_blk, prompt_keys, preferred_element_type=jnp.float32)
            * score_scale
        )
        own_scores = (
            jnp.einsum("qhd,kd->hqk", q_blk, k_blk, preferred_element_type=jnp.float32)
            * score_scale
        )
        allowed = (tag_blk[:, None] == tag_blk[None, :]) & (pos_blk[None, :] <= pos_blk[:, None])
        own_scores = jnp.where(allowed[None, :, :], own_scores, -jnp.inf)
        peak_score = jnp.maximum(
            jnp.max(cached_scores, axis=2, keepdims=True),
            jnp.max(own_scores, axis=2, keepdims=True),
        )
        cached_w = jnp.exp(cached_scores - peak_score)
        own_w = jnp.exp(own_scores - peak_score)
        weight_sum = jnp.sum(cached_w, axis=2) + jnp.sum(own_w, axis=2)
        summed = jnp.einsum(
            "hqk,kd->qhd",
            cached_w.astype(jnp.bfloat16),
            prompt_values,
            preferred_element_type=jnp.float32,
        )
        summed = summed + jnp.einsum(
            "hqk,kd->qhd", own_w.astype(jnp.bfloat16), v_blk, preferred_element_type=jnp.float32
        )
        result_blk = summed / jnp.transpose(weight_sum)[:, :, None]
        return result_blk.astype(jnp.bfloat16).reshape(q_blk.shape[0], head_cols)

    attended = lax.map(
        attend,
        (
            queries.reshape(block_count, block_rows, heads_here, head_size),
            keys_rot.reshape(block_count, block_rows, head_size),
            values_out.reshape(block_count, block_rows, head_size),
            slot_tags.reshape(block_count, block_rows),
            slot_pos.reshape(block_count, block_rows),
        ),
    )
    returned = lax.all_to_all(
        attended.reshape(rank_count, slot_size, head_cols),
        "dp",
        split_axis=0,
        concat_axis=0,
        tiled=True,
    )
    return jnp.take(returned.reshape(buffer_rows, head_cols), home_target, axis=0)


def solution(mesh):
    in_specs = (
        P(("group", "dp"), None),
        P(("group", "dp")),
        P(("group", "dp")),
        P(),
        P(None, "tensor"),
        P("tensor"),
        P(None, "tensor"),
        P("tensor"),
        P(None, "tensor"),
        P("tensor"),
        P(("group", "dp"), "tensor"),
        P(("group", "dp"), "tensor"),
    )
    out_specs = P(("group", "dp"), "tensor")
    return jax.shard_map(local, mesh=mesh, in_specs=in_specs, out_specs=out_specs, check_vma=False)
```

profile of v0, /device:TPU:0, one launch (start us, length us, event | category | flops | bytes accessed | tf_op | source)
XLA Modules:
  0.0 139.1 jit_solution(11629963594921517153)
XLA Ops:
  0.0 1.0 select_reduce_fusion.7
  2.7 0.9 convert_element_type.48
  3.7 3.1 %fusion.35 = f32[512]{0:T(512)S(1)} fusion(bf16[512,4096]{1,0:T(8,128)(2,1)} %param.14), kind=kLoop, calls=%fused_computation.41 | loop fusion | flops 6290944 | bytes 4196352 | tf_op jit(solution)/shard_map/reduce_sum | solution.py:67
  7.3 4.8 %convolution_add_fusion = f32[512,512]{0,1:T(8,128)S(1)} fusion(bf16[4096,512]{1,0:T(8,128)(2,1)} %param.18, f32[512]{0:T(512)S(1)} %convert_element_type.50, bf16[512,4096]{1,0:T(8,128)(2,1)S(1)} %copy-done.2, f32[4096]{0:T(1024)S(1)} %convert_element_type.48, f32[512]{0:T(512)S(1)} %add_rsqrt_fusion), kind=kOutput, calls=%fused_computation.45 | convolution fusion | flops 2156134400 | bytes 9457664 | tf_op jit(solution)/shard_map/dot_general | solution.py:69
  12.6 3.9 %fusion.38 = f32[512,1,128]{0,2,1:T(8,128)S(1)} fusion(bf16[4096,128]{1,0:T(8,128)(2,1)S(1)} %copy-done, f32[128]{0:T(128)S(1)} %convert_element_type.53, bf16[512,4096]{1,0:T(8,128)(2,1)} %param.14, f32[4096]{0:T(1024)S(1)} %convert_element_type.48, f32[512]{0:T(512)S(1)} %add_rsqrt_fusion), kind=kOutput, calls=%fused_computation.48 | convolution fusion | flops 545325056 | bytes 5523968 | tf_op jit(solution)/shard_map/dot_general | solution.py:72
  17.4 3.8 %fusion.39 = bf16[512,128]{0,1:T(8,128)(2,1)S(1)} fusion(bf16[4096,128]{1,0:T(8,128)(2,1)S(1)} %copy-done.8, f32[128]{0:T(128)S(1)} %convert_element_type.54, bf16[512,4096]{1,0:T(8,128)(2,1)} %param.14, f32[4096]{0:T(1024)S(1)} %convert_element_type.48, f32[512]{0:T(512)S(1)} %add_rsqrt_fusion), kind=kOutput, calls=%fused_computation.49 | convolution fusion | flops 545390592 | bytes 5392896 | tf_op jit(solution)/shard_map/dot_general | solution.py:75
  21.7 4.0 %gather_fusion = bf16[1024,768]{1,0:T(8,128)(2,1)S(1)} fusion(bf16[512,768]{1,0:T(8,128)(2,1)S(1)} %pad_maximum_fusion, s32[1024]{0:T(1024)S(1)} %broadcast_clamp_fusion), kind=kCustom, calls=%fused_computation | custom fusion | bytes 3149824 | tf_op jit(solution)/shard_map/jit(_take)/gather | solution.py:142
  25.8 1.4 select_select_fusion
  27.2 6.4 %all-to-all-start = ((bf16[4,256,768]{2,1,0:T(8,128)(2,1)}), bf16[4,256,768]{2,1,0:T(8,128)(2,1)}, u32[]{:S(2)}, u32[]{:S(2)}) async-start(bf16[4,256,768]{2,1,0:T(8,128)(2,1)} %select_select_fusion), calls=%async_computation | async-start | bytes 3145728 | tf_op jit(solution)/shard_map/all_to_all | solution.py:144
  35.3 35.5 %all-reduce.2 = (s32[32]{0:T(128)S(1)}, s32[32]{0:T(128)S(1)}) all-reduce(s32[32]{0:T(128)S(1)} %dynamic-update-slice.1, s32[32]{0:T(128)S(1)} %dynamic-update-slice), channel_id=1, replica_groups=mesh['group'=2,'dp'=4,'tensor'=4] {'dp'}, use_global_device_ids=true, to_apply=%add.1 | all-reduce | flops 64 | bytes 512
  71.9 1.3 slice.36
  73.2 1.8 %fusion.72 = (bf16[1024,128]{1,0:T(8,128)(2,1)}, bf16[1024,128]{1,0:T(8,128)(2,1)S(1)}) fusion(bf16[1024,768]{1,0:T(8,128)(2,1)} %bitcast.26), kind=kLoop, calls=%fused_computation.130 | loop fusion | bytes 1048576 | tf_op jit(solution)/shard_map/slice | solution.py:153
  74.9 1.1 reshape_reshape.2
  76.1 31.3 %while.10 = (s32[]{:T(128)}, bf16[2,512,512]{2,1,0:T(8,128)(2,1)}, bf16[2,512,4,128]{3,2,1,0:T(4,128)(2,1)}, bf16[2048,128]{1,0:T(8,128)(2,1)S(1)}, s32[2,512]{1...) while((s32[]{:T(128)}, bf16[2,512,512]{2,1,0:T(8,128)(2,1)}, ...), condition=%wide.region_17.18_spmd, body=%wide.region_12.17_spmd.sunk | while | flops 2731012096 | bytes 73274000 | solution.py:189
  76.3 1.2 constant_dynamic-slice_fusion.5
  77.6 0.9 fusion.89
  78.5 2.4 %bitcast_reduce_fusion.2 = (f32[4,512]{1,0:T(4,128)S(1)}, f32[512,4,2048]{2,0,1:T(8,128)S(1)}) fusion(bf16[2048,128]{1,0:T(8,128)(2,1)S(1)} %get-tuple-element.219, bf16[1,512,4,128]{3,2,1,0:T(4,128)(2,1)S(1)} %constant_dynamic-slice_fusion.5), kind=kOutput, calls=%fused_computation.3.clone.1 | convolution fusion | flops 1082128384 | bytes 17833984 | tf_op jit(solution)/shard_map/while/body/eval_jaxpr/qhd,kd->hqk/dot_general | solution.py:161
  80.9 0.9 fusion.92
  81.8 3.3 %fusion.91 = f32[4,512]{1,0:T(4,128)S(1)} fusion(f32[512,4,2048]{2,0,1:T(8,128)S(1)} %get-tuple-element.190, f32[4,512]{1,0:T(4,128)S(1)} %max.9), kind=kLoop, calls=%fused_computation.5.clone.1 | loop fusion | flops 12580864 | bytes 16793600 | tf_op jit(solution)/shard_map/while/body/eval_jaxpr/reduce_sum | solution.py:176
  85.1 4.2 %fusion.90 = f32[512,4,128]{0,2,1:T(8,128)S(1)} fusion(f32[512,4,2048]{2,0,1:T(8,128)S(1)} %get-tuple-element.190, f32[4,512]{1,0:T(4,128)S(1)} %max.9, bf16[2048,128]{0,1:T(8,128)(2,1)S(1)} %get-tuple-element.223), kind=kOutput, calls=%fused_computation.16.clone.1 | convolution fusion | flops 1086324736 | bytes 18358272 | tf_op jit(solution)/shard_map/while/body/eval_jaxpr/hqk,kd->qhd/dot_general | solution.py:177
  89.3 1.3 divide_convert_fusion.2
  92.0 1.2 constant_dynamic-slice_fusion.5
  93.2 0.9 fusion.89
  94.1 2.4 %bitcast_reduce_fusion.2 = (f32[4,512]{1,0:T(4,128)S(1)}, f32[512,4,2048]{2,0,1:T(8,128)S(1)}) fusion(bf16[2048,128]{1,0:T(8,128)(2,1)S(1)} %get-tuple-element.219, bf16[1,512,4,128]{3,2,1,0:T(4,128)(2,1)S(1)} %constant_dynamic-slice_fusion.5), kind=kOutput, calls=%fused_computation.3.clone.1 | convolution fusion | flops 1082128384 | bytes 17833984 | tf_op jit(solution)/shard_map/while/body/eval_jaxpr/qhd,kd->hqk/dot_general | solution.py:161
  96.6 0.9 fusion.92
  97.5 3.3 %fusion.91 = f32[4,512]{1,0:T(4,128)S(1)} fusion(f32[512,4,2048]{2,0,1:T(8,128)S(1)} %get-tuple-element.190, f32[4,512]{1,0:T(4,128)S(1)} %max.9), kind=kLoop, calls=%fused_computation.5.clone.1 | loop fusion | flops 12580864 | bytes 16793600 | tf_op jit(solution)/shard_map/while/body/eval_jaxpr/reduce_sum | solution.py:176
  100.8 4.2 %fusion.90 = f32[512,4,128]{0,2,1:T(8,128)S(1)} fusion(f32[512,4,2048]{2,0,1:T(8,128)S(1)} %get-tuple-element.190, f32[4,512]{1,0:T(4,128)S(1)} %max.9, bf16[2048,128]{0,1:T(8,128)(2,1)S(1)} %get-tuple-element.223), kind=kOutput, calls=%fused_computation.16.clone.1 | convolution fusion | flops 1086324736 | bytes 18358272 | tf_op jit(solution)/shard_map/while/body/eval_jaxpr/hqk,kd->qhd/dot_general | solution.py:177
  105.0 1.3 divide_convert_fusion.2
  107.4 3.5 %all-to-all-start.1 = ((bf16[4,256,512]{2,1,0:T(8,128)(2,1)}), bf16[4,256,512]{2,1,0:T(8,128)(2,1)S(1)}, u32[]{:S(2)}, u32[]{:S(2)}) async-start(bf16[4,256,512]{2,1,0:T(8,128)(2,1)} %bitcast.142), calls=%async_computation.1 | async-start | bytes 2097152 | tf_op jit(solution)/shard_map/all_to_all | solution.py:199
  111.0 25.2 %all-to-all-done.1 = bf16[4,256,512]{2,1,0:T(8,128)(2,1)S(1)} async-done(((bf16[4,256,512]{2,1,0:T(8,128)(2,1)}), bf16[4,256,512]{2,1,0:T(8,128)(2,1)S(1)}, u32[]{:S(2)}, u32[]{:S(2)}) %all-to-all-start.1) | async-done | bytes 1048608 | tf_op jit(solution)/shard_map/all_to_all | solution.py:199
  136.2 2.0 %gather_fusion.1 = bf16[512,512]{1,0:T(8,128)(2,1)S(1)} fusion(bf16[1024,512]{1,0:T(8,128)(2,1)S(1)} %bitcast.136, s32[1024]{0:T(1024)S(1)} %pad_clamp_fusion), kind=kCustom, calls=%fused_computation.1 | custom fusion | bytes 1050624 | tf_op jit(solution)/shard_map/jit(_take)/gather | solution.py:206
  138.1 0.9 broadcast_select_fusion
  (93 shorter events, 8.9 us)
Async XLA Ops:
  0.0 12.6 %copy-start = (bf16[4096,128]{1,0:T(8,128)(2,1)S(1)}, bf16[4096,128]{1,0:T(8,128)(2,1)}, u32[]{:S(2)}) copy-start(bf16[4096,128]{1,0:T(8,128)(2,1)} %param.20) | copy-start | bytes 3145732
  0.0 6.7 %copy-start.7 = (bf16[512]{0:T(512)(128)(2,1)S(1)}, bf16[512]{0:T(512)(128)(2,1)}, u32[]{:S(2)}) copy-start(bf16[512]{0:T(512)(128)(2,1)} %param.19) | copy-start | bytes 3076
  1.8 5.5 %copy-start.2 = (bf16[512,4096]{1,0:T(8,128)(2,1)S(1)}, bf16[512,4096]{1,0:T(8,128)(2,1)}, u32[]{:S(2)}) copy-start(bf16[512,4096]{1,0:T(8,128)(2,1)} %param.14) | copy-start | bytes 12582916
  7.3 5.3 %copy-start.9 = (bf16[128]{0:T(256)(128)(2,1)S(1)}, bf16[128]{0:T(256)(128)(2,1)}, u32[]{:S(2)}) copy-start(bf16[128]{0:T(256)(128)(2,1)} %param.21) | copy-start | bytes 772
  12.6 4.7 %copy-start.10 = (bf16[128]{0:T(256)(128)(2,1)S(1)}, bf16[128]{0:T(256)(128)(2,1)}, u32[]{:S(2)}) copy-start(bf16[128]{0:T(256)(128)(2,1)} %param.23) | copy-start | bytes 772
  12.6 4.7 %copy-start.8 = (bf16[4096,128]{1,0:T(8,128)(2,1)S(1)}, bf16[4096,128]{1,0:T(8,128)(2,1)}, u32[]{:S(2)}) copy-start(bf16[4096,128]{1,0:T(8,128)(2,1)} %param.22) | copy-start | bytes 3145732
  17.4 4.0 %copy-start.5 = (s32[8]{0:T(128)S(1)}, s32[8]{0:T(128)}, u32[]{:S(2)}) copy-start(s32[8]{0:T(128)} %param.16) | copy-start | bytes 100
  25.8 7.9 %copy-start.11 = (u32[32]{0:T(128)S(1)}, u32[32]{0:T(128)}, u32[]{:S(2)}) copy-start(u32[32]{0:T(128)} %constant.126) | copy-start | bytes 388
  25.8 9.4 %copy-start.6 = (s32[8]{0:T(128)S(1)}, s32[8]{0:T(128)}, u32[]{:S(2)}) copy-start(s32[8]{0:T(128)} %param.15) | copy-start | bytes 100
  25.8 45.8 %copy-start.3 = (bf16[2048,128]{1,0:T(8,128)(2,1)S(1)}, bf16[2048,128]{1,0:T(8,128)(2,1)}, u32[]{:S(2)}) copy-start(bf16[2048,128]{1,0:T(8,128)(2,1)} %param.25) | copy-start | bytes 1572868
  27.2 48.9 %copy-start.1 = (bf16[2048,128]{1,0:T(8,128)(2,1)S(1)}, bf16[2048,128]{1,0:T(8,128)(2,1)}, u32[]{:S(2)}) copy-start(bf16[2048,128]{1,0:T(8,128)(2,1)} %param.24) | copy-start | bytes 1572868
  27.2 44.7 %all-to-all-start = ((bf16[4,256,768]{2,1,0:T(8,128)(2,1)}), bf16[4,256,768]{2,1,0:T(8,128)(2,1)}, u32[]{:S(2)}, u32[]{:S(2)}) async-start(bf16[4,256,768]{2,1,0:T(8,128)(2,1)} %select_select_fusion), calls=%async_computation | async-start | bytes 3145728 | tf_op jit(solution)/shard_map/all_to_all | solution.py:144
  85.1 4.2 %copy-start.4 = (bf16[2,512,128]{2,1,0:T(8,128)(2,1)S(1)}, bf16[2,512,128]{2,1,0:T(8,128)(2,1)}, u32[]{:S(2)}) copy-start(bf16[2,512,128]{2,1,0:T(8,128)(2,1)} %get-tuple-element.224) | copy-start | bytes 786436 | tf_op jit(solution)/shard_map/while
  100.8 4.2 %copy-start.4 = (bf16[2,512,128]{2,1,0:T(8,128)(2,1)S(1)}, bf16[2,512,128]{2,1,0:T(8,128)(2,1)}, u32[]{:S(2)}) copy-start(bf16[2,512,128]{2,1,0:T(8,128)(2,1)} %get-tuple-element.224) | copy-start | bytes 786436 | tf_op jit(solution)/shard_map/while
  107.4 28.8 %all-to-all-start.1 = ((bf16[4,256,512]{2,1,0:T(8,128)(2,1)}), bf16[4,256,512]{2,1,0:T(8,128)(2,1)S(1)}, u32[]{:S(2)}, u32[]{:S(2)}) async-start(bf16[4,256,512]{2,1,0:T(8,128)(2,1)} %bitcast.142), calls=%async_computation.1 | async-start | bytes 2097152 | tf_op jit(solution)/shard_map/all_to_all | solution.py:199
where the time goes:
time: 140 us; the launch traced here: 139 us
  blocking collectives  35.5 us (25%)
  matrix products  30.1 us (22%)
  waiting for transfers between devices  25.2 us (18%)
  other arithmetic  20.2 us (14%)
  local copies, waits for them, and re-layouts  17 us (12%)
  starting transfers between devices  9.96 us (7%)
    unnamed x1, blocking collectives  35.5 us
    all_to_all x1, waiting for transfers between devices, local(): lax.all_to_all(attended.reshape(rank_count, slot_size, head_cols), 'dp',...  25.2 us
    reduce_sum x4, other arithmetic, attend(): weight_sum = jnp.sum(cached_w, axis=2) + jnp.sum(own_w, axis=2)  8.37 us
    dot_general x2, matrix products, attend(): jnp.einsum('hqk,kd->qhd', cached_w.astype(jnp.bfloat16), prompt_values, p...  8.34 us
    all_to_all x1, starting transfers between devices, local(): lax.all_to_all(filled.reshape(rank_count, slot_size, joined.shape[1]), 'd...  6.44 us
    dot_general x2, matrix products, attend(): jnp.einsum('qhd,kd->hqk', q_blk, prompt_keys, preferred_element_type=jnp....  4.86 us
    dot_general x1, matrix products, project(): jnp.dot(normed, q_weight, preferred_element_type=jnp.float32)  4.78 us
    gather x1, local copies, waits for them, and re-layouts, local(): picked = jnp.take(joined, send_rows, axis=0)  4 us
  transfers between devices with their start and end apart: 2, of which 1 were waited for; matrix products, arithmetic and copies ran while one was open for 1% of the time, Pallas kernels for 0%

commit v1 on v0

v1 whole, which is shorter than its diff:
```python
import functools
import math

import jax
import jax.numpy as jnp
from jax import lax
from jax.experimental import pallas as pl
from jax.experimental.pallas import tpu as pltpu
from jax.sharding import PartitionSpec as P

rope_base = 1000000.0
norm_eps = 1e-06
F32, BF16 = jnp.float32, jnp.bfloat16
MESH = pl.DeviceIdType.MESH
NT = (((1,), (1,)), ((), ()))


def kernel(
    n,
    len_ref,
    dest_ref,
    hidden_hbm,
    gain_ref,
    qw_hbm,
    qb_ref,
    kw_hbm,
    kb_ref,
    vw_hbm,
    vb_ref,
    pk_hbm,
    pv_hbm,
    table_ref,
    out_ref,
    hidden,
    normed,
    qw,
    kvw,
    pk,
    pv,
    queries,
    q_out,
    q_in,
    o_out,
    o_in,
    s_out,
    s_in,
    own_acc,
    own_stat,
    load_sem,
    q_send,
    q_recv,
    o_send,
    o_recv,
    s_send,
    s_recv,
):
    rows, feats = hidden.shape
    pairs, _, _, slot, hd = q_out.shape
    responses = len_ref.shape[0]
    factor = hd**-0.5 * math.log2(math.e)
    me = lax.axis_index("dp")

    loads = [
        pltpu.make_async_copy(hidden_hbm, hidden, load_sem.at[0]),
        pltpu.make_async_copy(qw_hbm, qw, load_sem.at[1]),
        pltpu.make_async_copy(kw_hbm, kvw.at[0], load_sem.at[2]),
        pltpu.make_async_copy(vw_hbm, kvw.at[1], load_sem.at[3]),
        pltpu.make_async_copy(pk_hbm, pk, load_sem.at[4]),
        pltpu.make_async_copy(pv_hbm, pv, load_sem.at[5]),
    ]
    for load in loads:
        load.start()

    barrier = pltpu.get_barrier_semaphore()
    for k in range(1, n):
        pl.semaphore_signal(
            barrier, inc=1, device_id={"dp": lax.rem(me + k, n)}, device_id_type=MESH
        )

    lengths = [len_ref[r] for r in range(responses)]
    dests = [dest_ref[r] for r in range(responses)]
    starts, shifts = [], []
    start = jnp.int32(0)
    for r in range(responses):
        offset = jnp.int32(0)
        for e in range(r):
            offset = offset + jnp.where(dests[e] == dests[r], lengths[e], 0)
        starts.append(start)
        shifts.append(dests[r] * slot + offset - start)
        start = start + lengths[r]

    def route(index):
        first = jnp.zeros_like(index)
        shift = jnp.zeros_like(index)
        for r in range(responses):
            reached = index >= starts[r]
            first = jnp.where(reached, starts[r], first)
            shift = jnp.where(reached, shifts[r], shift)
        return first, index + shift

    row_col = lax.broadcasted_iota(jnp.int32, (rows, 1), 0)
    first_col, target_col = route(row_col)
    _, target_row = route(lax.broadcasted_iota(jnp.int32, (1, rows), 1))

    spans = table_ref.shape[0]
    place_hot = (
        lax.broadcasted_iota(jnp.int32, (rows, spans), 1) == row_col - first_col
    ).astype(F32)
    turns = jnp.dot(
        place_hot, table_ref[...], precision=lax.Precision.HIGHEST, preferred_element_type=F32
    )
    cosine, sine = turns[:, :hd], turns[:, hd:]

    def rope(block):
        return (block * cosine + pltpu.roll(block, hd // 2, 1) * sine).astype(BF16)

    loads[0].wait()
    gain = gain_ref[...].astype(F32)
    step_rows = min(64, rows)

    def norm_step(i, carry):
        at = pl.ds(pl.multiple_of(i * step_rows, step_rows), step_rows)
        wide = hidden[at, :].astype(F32)
        scale = lax.rsqrt(jnp.mean(wide * wide, axis=1, keepdims=True) + norm_eps)
        normed[at, :] = (wide * scale * gain).astype(BF16)
        return carry

    lax.fori_loop(0, rows // step_rows, norm_step, 0)

    def q_copy(p, k):
        return pltpu.make_async_remote_copy(
            src_ref=q_out.at[p, k],
            dst_ref=q_in.at[p, k],
            send_sem=q_send.at[p, k],
            recv_sem=q_recv.at[p, k],
            device_id={"dp": lax.rem(me + k, n)},
            device_id_type=MESH,
        )

    def o_copy(p, k):
        return pltpu.make_async_remote_copy(
            src_ref=o_out.at[p, k],
            dst_ref=o_in.at[p, k],
            send_sem=o_send.at[p, k],
            recv_sem=o_recv.at[p, k],
            device_id={"dp": lax.rem(me - k + n, n)},
            device_id_type=MESH,
        )

    def s_copy(p, k):
        return pltpu.make_async_remote_copy(
            src_ref=s_out.at[p, k],
            dst_ref=s_in.at[p, k],
            send_sem=s_send.at[p, k],
            recv_sem=s_recv.at[p, k],
            device_id={"dp": lax.rem(me - k + n, n)},
            device_id_type=MESH,
        )

    order = [k for k in range(1, n) if k % 2 == 0] + [k for k in range(1, n) if k % 2] + [0]
    loads[1].wait()
    for p in range(pairs):
        cols = slice(p * 2 * hd, (p + 1) * 2 * hd)
        lin = jnp.dot(normed[...], qw[:, cols], preferred_element_type=F32)
        lin = lin + qb_ref[:, cols].astype(F32)
        both = jnp.concatenate([rope(lin[:, :hd]), rope(lin[:, hd:])], axis=1)
        queries[2 * p] = both[:, :hd]
        queries[2 * p + 1] = both[:, hd:]
        if p == 0:
            pl.semaphore_wait(barrier, n - 1)
        for k in order:
            base = lax.rem(me + k, n) * slot
            hot = lax.broadcasted_iota(jnp.int32, (slot, rows), 0) + base == target_row
            sent = jnp.dot(hot.astype(BF16), both, preferred_element_type=F32).astype(BF16)
            q_out[p, k, 0] = sent[:, :hd]
            q_out[p, k, 1] = sent[:, hd:]
            if k:
                q_copy(p, k).start()

    loads[2].wait()
    loads[3].wait()
    k_lin = jnp.dot(normed[...], kvw[0], preferred_element_type=F32) + kb_ref[...].astype(F32)
    keys = rope(k_lin)
    v_lin = jnp.dot(normed[...], kvw[1], preferred_element_type=F32) + vb_ref[...].astype(F32)
    values = v_lin.astype(BF16)
    col_row = lax.broadcasted_iota(jnp.int32, (rows, rows), 1)
    allowed = (col_row >= first_col) & (col_row <= row_col)
    stat_lane = lax.broadcasted_iota(jnp.int32, (rows, 128), 1)
    for h in range(2 * pairs):
        scores = lax.dot_general(queries[h], keys, NT, preferred_element_type=F32)
        scores = jnp.where(allowed, scores, -jnp.inf)
        peak = jnp.max(scores, axis=1, keepdims=True)
        weights = jnp.exp2((scores - peak) * factor)
        total = jnp.sum(weights, axis=1, keepdims=True)
        own_acc[h] = jnp.dot(weights.astype(BF16), values, preferred_element_type=F32)
        own_stat[h] = jnp.where(stat_lane == 0, peak, total)

    loads[4].wait()
    loads[5].wait()
    eye = (
        lax.broadcasted_iota(jnp.int32, (8, 128), 0) == lax.broadcasted_iota(jnp.int32, (8, 128), 1)
    ).astype(F32)
    lane = lax.broadcasted_iota(jnp.int32, (slot, 128), 1)

    def cached(p, k, source, o_to, s_to):
        stat = jnp.zeros((slot, 128), F32)
        for h in range(2):
            scores = lax.dot_general(source[p, k, h], pk[...], NT, preferred_element_type=F32)
            peak = jnp.max(scores, axis=1, keepdims=True)
            weights = jnp.exp2((scores - peak) * factor)
            total = jnp.sum(weights, axis=1, keepdims=True)
            summed = jnp.dot(weights.astype(BF16), pv[...], preferred_element_type=F32)
            o_to[p, k, h] = (summed / total).astype(BF16)
            stat = jnp.where(lane == 2 * h, peak, jnp.where(lane == 2 * h + 1, total, stat))
        s_to[p, k] = lax.dot_general(
            eye, stat, NT, precision=lax.Precision.HIGHEST, preferred_element_type=F32
        )

    def own_step(p, carry):
        cached(p, 0, q_out, o_in, s_in)
        return carry

    lax.fori_loop(0, pairs, own_step, 0)

    def away_step(i, carry):
        p = i // (n - 1)
        k = i % (n - 1) + 1
        q_copy(p, k).wait_recv()
        cached(p, k, q_in, o_out, s_out)
        o_copy(p, k).start()
        s_copy(p, k).start()
        return carry

    lax.fori_loop(0, pairs * (n - 1), away_step, 0)

    for p in range(pairs):
        gathered = jnp.zeros((rows, 2 * hd), F32)
        stat = jnp.zeros((rows, 8), F32)
        for k in [0] + list(range(1, n)):
            if k:
                o_copy(p, k).wait_recv()
                s_copy(p, k).wait_recv()
            base = lax.rem(me + k, n) * slot
            hot = lax.broadcasted_iota(jnp.int32, (rows, slot), 1) + base == target_col
            block = jnp.concatenate([o_in[p, k, 0], o_in[p, k, 1]], axis=1)
            gathered += jnp.dot(hot.astype(BF16), block, preferred_element_type=F32)
            stat += lax.dot_general(
                hot.astype(F32),
                s_in[p, k],
                NT,
                precision=lax.Precision.HIGHEST,
                preferred_element_type=F32,
            )
        for h in range(2):
            head = 2 * p + h
            peak, total = stat[:, 2 * h : 2 * h + 1], stat[:, 2 * h + 1 : 2 * h + 2]
            own_peak, own_total = own_stat[head][:, 0:1], own_stat[head][:, 1:2]
            top = jnp.maximum(peak, own_peak)
            far = jnp.exp2((peak - top) * factor) * total
            near = jnp.exp2((own_peak - top) * factor)
            mixed = gathered[:, h * hd : (h + 1) * hd] * far + own_acc[head] * near
            out_ref[:, head * hd : (head + 1) * hd] = (
                mixed / (far + near * own_total)
            ).astype(BF16)

    for p in range(pairs):
        for k in range(1, n):
            q_copy(p, k).wait_send()
            o_copy(p, k).wait_send()
            s_copy(p, k).wait_send()


def local(
    hidden,
    lengths,
    assignment,
    norm_gain,
    q_weight,
    q_bias,
    k_weight,
    k_bias,
    v_weight,
    v_bias,
    prompt_keys,
    prompt_values,
):
    n = lax.axis_size("dp")
    rows, feats = hidden.shape
    slot = 2 * rows // n
    hd = k_weight.shape[1]
    cols = q_weight.shape[1]
    pairs = cols // hd // 2
    plen = prompt_keys.shape[0]
    half = hd // 2
    freqs = rope_base ** (-(jnp.arange(half, dtype=F32) * 2.0) / hd)
    position = plen + jnp.arange(slot, dtype=jnp.int32)
    angles = position.astype(F32)[:, None] * freqs[None, :]
    cosine, sine = jnp.cos(angles), jnp.sin(angles)
    table = jnp.concatenate([cosine, cosine, -sine, sine], axis=1)
    smem = pl.BlockSpec(memory_space=pltpu.SMEM)
    vmem = pl.BlockSpec(memory_space=pltpu.VMEM)
    hbm = pl.BlockSpec(memory_space=pl.ANY)
    dma = pltpu.SemaphoreType.DMA
    flops = 2 * rows * feats * (cols + 2 * hd) + 8 * rows * cols * plen
    return pl.pallas_call(
        functools.partial(kernel, n),
        out_shape=jax.ShapeDtypeStruct((rows, cols), BF16),
        in_specs=[smem, smem, hbm, vmem, hbm, vmem, hbm, vmem, hbm, vmem, hbm, hbm, vmem],
        out_specs=vmem,
        scratch_shapes=[
            pltpu.VMEM((rows, feats), BF16),
            pltpu.VMEM((rows, feats), BF16),
            pltpu.VMEM((feats, cols), BF16),
            pltpu.VMEM((2, feats, hd), BF16),
            pltpu.VMEM((plen, hd), BF16),
            pltpu.VMEM((plen, hd), BF16),
            pltpu.VMEM((2 * pairs, rows, hd), BF16),
            pltpu.VMEM((pairs, n, 2, slot, hd), BF16),
            pltpu.VMEM((pairs, n, 2, slot, hd), BF16),
            pltpu.VMEM((pairs, n, 2, slot, hd), BF16),
            pltpu.VMEM((pairs, n, 2, slot, hd), BF16),
            pltpu.VMEM((pairs, n, 8, slot), F32),
            pltpu.VMEM((pairs, n, 8, slot), F32),
            pltpu.VMEM((2 * pairs, rows, hd), F32),
            pltpu.VMEM((2 * pairs, rows, 128), F32),
            dma((6,)),
            dma((pairs, n)),
            dma((pairs, n)),
            dma((pairs, n)),
            dma((pairs, n)),
            dma((pairs, n)),
            dma((pairs, n)),
        ],
        compiler_params=pltpu.CompilerParams(
            collective_id=0, has_side_effects=True, vmem_limit_bytes=56 * 1024 * 1024
        ),
        cost_estimate=pl.CostEstimate(
            flops=flops, bytes_accessed=rows * feats * 6, transcendentals=2 * rows * plen * 4
        ),
    )(
        lengths,
        assignment,
        hidden,
        norm_gain.reshape(1, -1),
        q_weight,
        q_bias.reshape(1, -1),
        k_weight,
        k_bias.reshape(1, -1),
        v_weight,
        v_bias.reshape(1, -1),
        prompt_keys,
        prompt_values,
        table,
    )


def solution(mesh):
    in_specs = (
        P(("group", "dp"), None),
        P(("group", "dp")),
        P(("group", "dp")),
        P(),
        P(None, "tensor"),
        P("tensor"),
        P(None, "tensor"),
        P("tensor"),
        P(None, "tensor"),
        P("tensor"),
        P(("group", "dp"), "tensor"),
        P(("group", "dp"), "tensor"),
    )
    out_specs = P(("group", "dp"), "tensor")
    return jax.shard_map(
        local, mesh=mesh, in_specs=in_specs, out_specs=out_specs, check_vma=False
    )
```

time: 140 us -> 69.5 us (0.50)
  Pallas kernels: 0 us -> 63.4 us
  blocking collectives: 35.5 us -> 0 us
  matrix products: 30.1 us -> 0 us
  waiting for transfers between devices: 25.2 us -> 0 us
  other arithmetic: 20.2 us -> 1.43 us
  local copies, waits for them, and re-layouts: 17 us -> 4.44 us
  starting transfers between devices: 9.96 us -> 0 us
    pallas_call x0 -> x1, Pallas kernels: none -> 63.4 us  [local(): pl.pallas_call(functools.partial(kernel, n), out_shape=jax.ShapeDtypeStru...]
    unnamed x1 -> x0, blocking collectives: 35.5 us -> none
    dot_general x11 -> x0, matrix products: 30.1 us -> none  [the longest x2 8.34 us: attend(): jnp.einsum('hqk,kd->qhd', cached_w.astype(jnp.bfloat16), prompt_values, p...]
    all_to_all x2 -> x0, waiting for transfers between devices: 25.2 us -> none  [the longest x1 25.2 us: local(): lax.all_to_all(attended.reshape(rank_count, slot_size, head_cols), 'dp',...]
    reduce_sum x10 -> x0, other arithmetic: 12.9 us -> none  [the longest x4 8.37 us: attend(): weight_sum = jnp.sum(cached_w, axis=2) + jnp.sum(own_w, axis=2)]
    all_to_all x2 -> x0, starting transfers between devices: 9.96 us -> none  [the longest x1 6.44 us: local(): lax.all_to_all(filled.reshape(rank_count, slot_size, joined.shape[1]), 'd...]
    gather x2 -> x0, local copies, waits for them, and re-layouts: 5.97 us -> none  [the longest x1 4 us: local(): picked = jnp.take(joined, send_rows, axis=0)]
    slice x2 -> x0, local copies, waits for them, and re-layouts: 3.07 us -> none  [the longest x1 1.78 us: local(): values_out = arrived[:, head_cols + head_size:]]
  transfers between devices with their start and end apart: 2 -> 0, of which waited for: 1 -> 0; matrix products, arithmetic and copies ran while one was open for 1% -> 0% of each run, Pallas kernels for 0% -> 0%
where the time goes in v1:
time: 69.5 us; the launch traced here: 69.3 us
  Pallas kernels  63.4 us (91%)
  local copies, waits for them, and re-layouts  4.44 us (6%)
  other arithmetic  1.43 us (2%)
    pallas_call x1, Pallas kernels, local(): pl.pallas_call(functools.partial(kernel, n), out_shape=jax.ShapeDtypeStru...  63.4 us
    unnamed x1, local copies, waits for them, and re-layouts  1.87 us

profile of v1, /device:TPU:0, one launch (start us, length us, event | category | flops | bytes accessed | tf_op | source)
XLA Modules:
  0.0 69.3 jit_solution(4353831431279949051)
XLA Ops:
  0.0 1.3 %reshape.25.qb_ref = bf16[1,512]{1,0:T(2,128)(2,1)} reshape(bf16[512]{0:T(512)(128)(2,1)} %param.17) | data formatting | bytes 2048 | tf_op jit(solution)/shard_map/reshape | solution.py:346
  1.3 1.3 %reshape.24.gain_ref = bf16[1,4096]{1,0:T(2,128)(2,1)} reshape(bf16[4096]{0:T(1024)(128)(2,1)} %param.15) | data formatting | bytes 16384 | tf_op jit(solution)/shard_map/reshape | solution.py:344
  2.6 0.5 multiply_cosine_fusion
  3.1 0.9 %pad_maximum_fusion.table_ref = f32[256,256]{1,0:T(8,128)} fusion(f32[256,64]{1,0:T(8,128)S(1)} %get-tuple-element.7, f32[256,64]{1,0:T(8,128)S(1)} %get-tuple-element.6, f32[256,64]{1,0:T(8,128)S(1)} %get-tuple-element.5), kind=kLoop, calls=%fused_computation | loop fusion | flops 196608 | bytes 458752 | tf_op jit(solution)/shard_map/concatenate | solution.py:299
  4.0 63.4 %shard_map.118 = bf16[512,512]{1,0:T(8,128)(2,1)} custom-call(s32[8]{0:T(128)} %len_ref.1, s32[8]{0:T(128)} %dest_ref.1, bf16[512,4096]{1,0:T(8,128)(2,1)} %hidden_hbm.1, bf16[1,4096]{1,0:T(2,128)(2,1)} %reshape.24.gain_ref, bf16[4096,512]{1,0:T(8,128)(2,1)} %qw_hbm.1, bf16[1,512]{1,0:T(2,128)(2,1)} %reshape.25.qb_ref, bf16[4096,128]{1,0:T(8,128)(2,1)} %kw_hbm.1, ...), custom_call_target="tpu_custom_call" | custom-call | flops 7516192768 | bytes 12582912 | tf_op jit(solution)/shard_map/pallas_call | solution.py:305
  67.4 1.9 %copy.15 = bf16[512,512]{1,0:T(8,128)(2,1)} copy(bf16[512,512]{1,0:T(8,128)(2,1)} %shard_map.118) | data formatting | bytes 1048576
  (2 shorter events, 0.0 us)

commit v2 on v1

--- a/solution.py
+++ b/solution.py
@@ -29,7 +29,8 @@
     vb_ref,
     pk_hbm,
     pv_hbm,
-    table_ref,
+    cos_ref,
+    sin_ref,
     out_ref,
     hidden,
     normed,
@@ -47,6 +48,8 @@
     own_acc,
     own_stat,
     load_sem,
+    hidden_sem,
+    qw_sem,
     q_send,
     q_recv,
     o_send,
@@ -60,15 +63,24 @@
     factor = hd**-0.5 * math.log2(math.e)
     me = lax.axis_index("dp")
 
-    loads = [
-        pltpu.make_async_copy(hidden_hbm, hidden, load_sem.at[0]),
-        pltpu.make_async_copy(qw_hbm, qw, load_sem.at[1]),
-        pltpu.make_async_copy(kw_hbm, kvw.at[0], load_sem.at[2]),
-        pltpu.make_async_copy(vw_hbm, kvw.at[1], load_sem.at[3]),
-        pltpu.make_async_copy(pk_hbm, pk, load_sem.at[4]),
-        pltpu.make_async_copy(pv_hbm, pv, load_sem.at[5]),
+    chunk = min(128, rows)
+    chunks = [slice(c * chunk, (c + 1) * chunk) for c in range(rows // chunk)]
+    hidden_loads = [
+        pltpu.make_async_copy(hidden_hbm.at[at], hidden.at[at], hidden_sem.at[c])
+        for c, at in enumerate(chunks)
     ]
-    for load in loads:
+    pair_cols = [slice(p * 2 * hd, (p + 1) * 2 * hd) for p in range(pairs)]
+    qw_loads = [
+        pltpu.make_async_copy(qw_hbm.at[:, at], qw.at[:, at], qw_sem.at[p])
+        for p, at in enumerate(pair_cols)
+    ]
+    loads = qw_loads[1:] + [
+        pltpu.make_async_copy(kw_hbm, kvw.at[0], load_sem.at[0]),
+        pltpu.make_async_copy(vw_hbm, kvw.at[1], load_sem.at[1]),
+        pltpu.make_async_copy(pk_hbm, pk, load_sem.at[2]),
+        pltpu.make_async_copy(pv_hbm, pv, load_sem.at[3]),
+    ]
+    for load in hidden_loads + qw_loads[:1]:
         load.start()
 
     barrier = pltpu.get_barrier_semaphore()
@@ -76,6 +88,21 @@
         pl.semaphore_signal(
             barrier, inc=1, device_id={"dp": lax.rem(me + k, n)}, device_id_type=MESH
         )
+
+    paired = n & (n - 1) == 0 and n <= 4
+
+    def toggled(k):
+        index = me
+        for bit in (1, 2):
+            if k & bit:
+                index = index + bit - 2 * bit * ((me // bit) % 2)
+        return index
+
+    def target_of(k):
+        return toggled(k) if paired else lax.rem(me + k, n)
+
+    def origin_of(k):
+        return toggled(k) if paired else lax.rem(me - k + n, n)
 
     lengths = [len_ref[r] for r in range(responses)]
     dests = [dest_ref[r] for r in range(responses)]
@@ -102,30 +129,39 @@
     first_col, target_col = route(row_col)
     _, target_row = route(lax.broadcasted_iota(jnp.int32, (1, rows), 1))
 
-    spans = table_ref.shape[0]
+    spans = cos_ref.shape[0]
     place_hot = (
         lax.broadcasted_iota(jnp.int32, (rows, spans), 1) == row_col - first_col
     ).astype(F32)
-    turns = jnp.dot(
-        place_hot, table_ref[...], precision=lax.Precision.HIGHEST, preferred_element_type=F32
-    )
-    cosine, sine = turns[:, :hd], turns[:, hd:]
+    def turn(ref):
+        return jnp.dot(
+            place_hot, ref[...], precision=lax.Precision.HIGHEST, preferred_element_type=F32
+        )
+
+    cos_half, sin_half = turn(cos_ref), turn(sin_ref)
+    cosine = jnp.concatenate([cos_half, cos_half], axis=1)
+    sine = jnp.concatenate([-sin_half, sin_half], axis=1)
 
     def rope(block):
         return (block * cosine + pltpu.roll(block, hd // 2, 1) * sine).astype(BF16)
 
-    loads[0].wait()
-    gain = gain_ref[...].astype(F32)
-    step_rows = min(64, rows)
-
-    def norm_step(i, carry):
-        at = pl.ds(pl.multiple_of(i * step_rows, step_rows), step_rows)
+    gain = gain_ref[...].astype(F32).reshape(1, feats)
+    q_bias = qb_ref[...].astype(F32).reshape(1, 2 * pairs * hd)
+    k_bias = kb_ref[...].astype(F32).reshape(1, hd)
+    v_bias = vb_ref[...].astype(F32).reshape(1, hd)
+    first_lin = []
+    for c, at in enumerate(chunks):
+        hidden_loads[c].wait()
         wide = hidden[at, :].astype(F32)
         scale = lax.rsqrt(jnp.mean(wide * wide, axis=1, keepdims=True) + norm_eps)
         normed[at, :] = (wide * scale * gain).astype(BF16)
-        return carry
-
-    lax.fori_loop(0, rows // step_rows, norm_step, 0)
+        if c == 0:
+            qw_loads[0].wait()
+        first_lin.append(
+            jnp.dot(normed[at, :], qw[:, pair_cols[0]], preferred_element_type=F32)
+        )
+    for load in loads:
+        load.start()
 
     def q_copy(p, k):
         return pltpu.make_async_remote_copy(
@@ -133,7 +169,7 @@
             dst_ref=q_in.at[p, k],
             send_sem=q_send.at[p, k],
             recv_sem=q_recv.at[p, k],
-            device_id={"dp": lax.rem(me + k, n)},
+            device_id={"dp": target_of(k)},
             device_id_type=MESH,
         )
 
@@ -143,7 +179,7 @@
             dst_ref=o_in.at[p, k],
             send_sem=o_send.at[p, k],
             recv_sem=o_recv.at[p, k],
-            device_id={"dp": lax.rem(me - k + n, n)},
+            device_id={"dp": origin_of(k)},
             device_id_type=MESH,
         )
 
@@ -153,23 +189,26 @@
             dst_ref=s_in.at[p, k],
             send_sem=s_send.at[p, k],
             recv_sem=s_recv.at[p, k],
-            device_id={"dp": lax.rem(me - k + n, n)},
+            device_id={"dp": origin_of(k)},
             device_id_type=MESH,
         )
 
-    order = [k for k in range(1, n) if k % 2 == 0] + [k for k in range(1, n) if k % 2] + [0]
-    loads[1].wait()
+    order = ([2, 3, 1] if paired and n == 4 else list(range(1, n))) + [0]
     for p in range(pairs):
-        cols = slice(p * 2 * hd, (p + 1) * 2 * hd)
-        lin = jnp.dot(normed[...], qw[:, cols], preferred_element_type=F32)
-        lin = lin + qb_ref[:, cols].astype(F32)
+        cols = pair_cols[p]
+        if p:
+            qw_loads[p].wait()
+            lin = jnp.dot(normed[...], qw[:, cols], preferred_element_type=F32)
+        else:
+            lin = jnp.concatenate(first_lin, axis=0)
+        lin = lin + q_bias[:, cols]
         both = jnp.concatenate([rope(lin[:, :hd]), rope(lin[:, hd:])], axis=1)
         queries[2 * p] = both[:, :hd]
         queries[2 * p + 1] = both[:, hd:]
         if p == 0:
             pl.semaphore_wait(barrier, n - 1)
         for k in order:
-            base = lax.rem(me + k, n) * slot
+            base = target_of(k) * slot
             hot = lax.broadcasted_iota(jnp.int32, (slot, rows), 0) + base == target_row
             sent = jnp.dot(hot.astype(BF16), both, preferred_element_type=F32).astype(BF16)
             q_out[p, k, 0] = sent[:, :hd]
@@ -177,11 +216,12 @@
             if k:
                 q_copy(p, k).start()
 
-    loads[2].wait()
-    loads[3].wait()
-    k_lin = jnp.dot(normed[...], kvw[0], preferred_element_type=F32) + kb_ref[...].astype(F32)
+    loads = loads[pairs - 1 :]
+    loads[0].wait()
+    loads[1].wait()
+    k_lin = jnp.dot(normed[...], kvw[0], preferred_element_type=F32) + k_bias
     keys = rope(k_lin)
-    v_lin = jnp.dot(normed[...], kvw[1], preferred_element_type=F32) + vb_ref[...].astype(F32)
+    v_lin = jnp.dot(normed[...], kvw[1], preferred_element_type=F32) + v_bias
     values = v_lin.astype(BF16)
     col_row = lax.broadcasted_iota(jnp.int32, (rows, rows), 1)
     allowed = (col_row >= first_col) & (col_row <= row_col)
@@ -195,8 +235,8 @@
         own_acc[h] = jnp.dot(weights.astype(BF16), values, preferred_element_type=F32)
         own_stat[h] = jnp.where(stat_lane == 0, peak, total)
 
-    loads[4].wait()
-    loads[5].wait()
+    loads[2].wait()
+    loads[3].wait()
     eye = (
         lax.broadcasted_iota(jnp.int32, (8, 128), 0) == lax.broadcasted_iota(jnp.int32, (8, 128), 1)
     ).astype(F32)
@@ -222,25 +262,31 @@
 
     lax.fori_loop(0, pairs, own_step, 0)
 
-    def away_step(i, carry):
-        p = i // (n - 1)
-        k = i % (n - 1) + 1
+    def away(p, k):
         q_copy(p, k).wait_recv()
         cached(p, k, q_in, o_out, s_out)
+        s_copy(p, k).start()
         o_copy(p, k).start()
-        s_copy(p, k).start()
+
+    def away_step(i, carry):
+        away(i // (n - 1), i % (n - 1) + 1)
         return carry
 
-    lax.fori_loop(0, pairs * (n - 1), away_step, 0)
+    if paired:
+        for p in range(pairs):
+            for k in order[:-1]:
+                away(p, k)
+    else:
+        lax.fori_loop(0, pairs * (n - 1), away_step, 0)
 
     for p in range(pairs):
         gathered = jnp.zeros((rows, 2 * hd), F32)
         stat = jnp.zeros((rows, 8), F32)
-        for k in [0] + list(range(1, n)):
+        for k in order[-1:] + order[:-1]:
             if k:
+                s_copy(p, k).wait_recv()
                 o_copy(p, k).wait_recv()
-                s_copy(p, k).wait_recv()
-            base = lax.rem(me + k, n) * slot
+            base = target_of(k) * slot
             hot = lax.broadcasted_iota(jnp.int32, (rows, slot), 1) + base == target_col
             block = jnp.concatenate([o_in[p, k, 0], o_in[p, k, 1]], axis=1)
             gathered += jnp.dot(hot.astype(BF16), block, preferred_element_type=F32)
@@ -295,8 +341,6 @@
     freqs = rope_base ** (-(jnp.arange(half, dtype=F32) * 2.0) / hd)
     position = plen + jnp.arange(slot, dtype=jnp.int32)
     angles = position.astype(F32)[:, None] * freqs[None, :]
-    cosine, sine = jnp.cos(angles), jnp.sin(angles)
-    table = jnp.concatenate([cosine, cosine, -sine, sine], axis=1)
     smem = pl.BlockSpec(memory_space=pltpu.SMEM)
     vmem = pl.BlockSpec(memory_space=pltpu.VMEM)
     hbm = pl.BlockSpec(memory_space=pl.ANY)
@@ -305,7 +349,7 @@
     return pl.pallas_call(
         functools.partial(kernel, n),
         out_shape=jax.ShapeDtypeStruct((rows, cols), BF16),
-        in_specs=[smem, smem, hbm, vmem, hbm, vmem, hbm, vmem, hbm, vmem, hbm, hbm, vmem],
+        in_specs=[smem, smem, hbm, vmem, hbm, vmem, hbm, vmem, hbm, vmem, hbm, hbm, vmem, vmem],
         out_specs=vmem,
         scratch_shapes=[
             pltpu.VMEM((rows, feats), BF16),
@@ -323,7 +367,9 @@
             pltpu.VMEM((pairs, n, 8, slot), F32),
             pltpu.VMEM((2 * pairs, rows, hd), F32),
             pltpu.VMEM((2 * pairs, rows, 128), F32),
-            dma((6,)),
+            dma((4,)),
+            dma((max(1, rows // min(128, rows)),)),
+            dma((pairs,)),
             dma((pairs, n)),
             dma((pairs, n)),
             dma((pairs, n)),
@@ -341,16 +387,17 @@
         lengths,
         assignment,
         hidden,
-        norm_gain.reshape(1, -1),
+        norm_gain,
         q_weight,
-        q_bias.reshape(1, -1),
+        q_bias,
         k_weight,
-        k_bias.reshape(1, -1),
+        k_bias,
         v_weight,
-        v_bias.reshape(1, -1),
+        v_bias,
         prompt_keys,
         prompt_values,
-        table,
+        jnp.cos(angles),
+        jnp.sin(angles),
     )
 
 

time: 69.5 us -> 66.2 us (0.953)
  local copies, waits for them, and re-layouts: 4.44 us -> 1.87 us
    reshape x2 -> x0, local copies, waits for them, and re-layouts: 2.57 us -> none  [the longest x1 1.31 us: local(): norm_gain.reshape(1, -1)]
    sin x0 -> x1, other arithmetic: none -> 1.24 us  [local(): jnp.sin(angles)]
    concatenate x1 -> x0, other arithmetic: 0.88 us -> none  [local(): table = jnp.concatenate([cosine, cosine, -sine, sine], axis=1)]
where the time goes in v2:
time: 66.2 us; the launch traced here: 66 us
  Pallas kernels  62.9 us (95%)
  local copies, waits for them, and re-layouts  1.87 us (3%)
  other arithmetic  1.25 us (2%)
    pallas_call x1, Pallas kernels, local(): pl.pallas_call(functools.partial(kernel, n), out_shape=jax.ShapeDtypeStru...  62.9 us
    unnamed x1, local copies, waits for them, and re-layouts  1.87 us

profile of v2, /device:TPU:0, one launch (start us, length us, event | category | flops | bytes accessed | tf_op | source)
XLA Modules:
  0.0 66.0 jit_solution(13349288508590372356)
XLA Ops:
  0.0 1.2 %multiply_sine_fusion = (f32[256,64]{1,0:T(8,128)}, f32[256,64]{1,0:T(8,128)}) fusion(f32[64]{0:T(128)S(1)} %multiply_power_fusion, f32[256]{0:T(256)S(1)} %add_convert_fusion), kind=kLoop, calls=%fused_computation | loop fusion | flops 16384 | bytes 132352 | tf_op jit(solution)/shard_map/sin | solution.py:400
  1.3 62.9 %shard_map.118 = bf16[512,512]{1,0:T(8,128)(2,1)} custom-call(s32[8]{0:T(128)} %len_ref.1, s32[8]{0:T(128)} %dest_ref.1, bf16[512,4096]{1,0:T(8,128)(2,1)} %hidden_hbm.1, bf16[4096]{0:T(1024)(128)(2,1)} %gain_ref.1, bf16[4096,512]{1,0:T(8,128)(2,1)} %qw_hbm.1, bf16[512]{0:T(512)(128)(2,1)} %qb_ref.1, bf16[4096,128]{1,0:T(8,128)(2,1)} %kw_hbm.1, ...), custom_call_target="tpu_custom_call" | custom-call | flops 7516192768 | bytes 12582912 | tf_op jit(solution)/shard_map/pallas_call | solution.py:349
  64.1 1.9 %copy.14 = bf16[512,512]{1,0:T(8,128)(2,1)} copy(bf16[512,512]{1,0:T(8,128)(2,1)} %shard_map.118) | data formatting | bytes 1048576
  (2 shorter events, 0.0 us)

commit v3 on v2

--- a/solution.py
+++ b/solution.py
@@ -279,24 +279,23 @@
     else:
         lax.fori_loop(0, pairs * (n - 1), away_step, 0)
 
+    def home_hot(k):
+        slots = lax.broadcasted_iota(jnp.int32, (rows, slot), 1) + target_of(k) * slot
+        return slots == target_col
+
     for p in range(pairs):
-        gathered = jnp.zeros((rows, 2 * hd), F32)
         stat = jnp.zeros((rows, 8), F32)
-        for k in order[-1:] + order[:-1]:
+        for k in order[::-1]:
             if k:
                 s_copy(p, k).wait_recv()
-                o_copy(p, k).wait_recv()
-            base = target_of(k) * slot
-            hot = lax.broadcasted_iota(jnp.int32, (rows, slot), 1) + base == target_col
-            block = jnp.concatenate([o_in[p, k, 0], o_in[p, k, 1]], axis=1)
-            gathered += jnp.dot(hot.astype(BF16), block, preferred_element_type=F32)
             stat += lax.dot_general(
-                hot.astype(F32),
+                home_hot(k).astype(F32),
                 s_in[p, k],
                 NT,
                 precision=lax.Precision.HIGHEST,
                 preferred_element_type=F32,
             )
+        shares, rests = [], []
         for h in range(2):
             head = 2 * p + h
             peak, total = stat[:, 2 * h : 2 * h + 1], stat[:, 2 * h + 1 : 2 * h + 2]
@@ -304,9 +303,19 @@
             top = jnp.maximum(peak, own_peak)
             far = jnp.exp2((peak - top) * factor) * total
             near = jnp.exp2((own_peak - top) * factor)
-            mixed = gathered[:, h * hd : (h + 1) * hd] * far + own_acc[head] * near
+            whole = far + near * own_total
+            shares.append(jnp.broadcast_to(far / whole, (rows, hd)))
+            rests.append(own_acc[head] * (near / whole))
+        gathered = jnp.zeros((rows, 2 * hd), F32)
+        for k in order[-1:] + order[-2::-1][:1] + order[:-2]:
+            if k:
+                o_copy(p, k).wait_recv()
+            block = jnp.concatenate([o_in[p, k, 0], o_in[p, k, 1]], axis=1)
+            gathered += jnp.dot(home_hot(k).astype(BF16), block, preferred_element_type=F32)
+        for h in range(2):
+            head = 2 * p + h
             out_ref[:, head * hd : (head + 1) * hd] = (
-                mixed / (far + near * own_total)
+                gathered[:, h * hd : (h + 1) * hd] * shares[h] + rests[h]
             ).astype(BF16)
 
     for p in range(pairs):

time: 66.2 us -> 63.5 us (0.959)
  Pallas kernels: 62.9 us -> 60 us
    pallas_call x1, Pallas kernels: 62.9 us -> 60 us  [local(): pl.pallas_call(functools.partial(kernel, n), out_shape=jax.ShapeDtypeStru...]
where the time goes in v3:
time: 63.5 us; the launch traced here: 63.1 us
  Pallas kernels  60 us (94%)
  local copies, waits for them, and re-layouts  1.87 us (3%)
  other arithmetic  1.25 us (2%)
    pallas_call x1, Pallas kernels, local(): pl.pallas_call(functools.partial(kernel, n), out_shape=jax.ShapeDtypeStru...  60 us
    unnamed x1, local copies, waits for them, and re-layouts  1.87 us

profile of v3, /device:TPU:0, one launch (start us, length us, event | category | flops | bytes accessed | tf_op | source)
XLA Modules:
  0.0 63.1 jit_solution(12451048703768169435)
XLA Ops:
  0.0 1.2 %multiply_sine_fusion = (f32[256,64]{1,0:T(8,128)}, f32[256,64]{1,0:T(8,128)}) fusion(f32[64]{0:T(128)S(1)} %multiply_power_fusion, f32[256]{0:T(256)S(1)} %add_convert_fusion), kind=kLoop, calls=%fused_computation | loop fusion | flops 16384 | bytes 132352 | tf_op jit(solution)/shard_map/sin | solution.py:409
  1.3 60.0 %shard_map.118 = bf16[512,512]{1,0:T(8,128)(2,1)} custom-call(s32[8]{0:T(128)} %len_ref.1, s32[8]{0:T(128)} %dest_ref.1, bf16[512,4096]{1,0:T(8,128)(2,1)} %hidden_hbm.1, bf16[4096]{0:T(1024)(128)(2,1)} %gain_ref.1, bf16[4096,512]{1,0:T(8,128)(2,1)} %qw_hbm.1, bf16[512]{0:T(512)(128)(2,1)} %qb_ref.1, bf16[4096,128]{1,0:T(8,128)(2,1)} %kw_hbm.1, ...), custom_call_target="tpu_custom_call" | custom-call | flops 7516192768 | bytes 12582912 | tf_op jit(solution)/shard_map/pallas_call | solution.py:358
  61.2 1.9 %copy.14 = bf16[512,512]{1,0:T(8,128)(2,1)} copy(bf16[512,512]{1,0:T(8,128)(2,1)} %shard_map.118) | data formatting | bytes 1048576
  (2 shorter events, 0.0 us)
